TPU v7x, 256 devices: a whole 4x4x8 slice. The times are simulated.
256 devices in a mesh: va: 8 (over z_hi, y), vb: 4 (over z_lo), oj: 8 (over x, core).
Axes of the slice: x: 4, y: 4, z: 8 (z_hi: 2, z_lo: 4; z = z_hi * 4 + z_lo), core: 2. Of those that a mesh axis runs over, the one named last changes fastest.
Arguments:
- occ_slab: bfloat16 [3584, 2, 2048], P(('vb', 'oj'), None, 'va'), may hold values from -0.875 to 0.875
- pair_slab: bfloat16 [3584, 8, 2048], P(('va', 'oj'), None, 'vb'), may hold values from -0.875 to 0.875
- occ_energy: float32 [2], replicated, may hold values from -1.5 to -0.3
- pair_energy: float32 [8], P('oj'), may hold values from -1.5 to -0.3
- vir_energy: float32 [2048], replicated, may hold values from 0.2 to 3
Outputs:
- gamma_occ: float32 [3584, 2, 2048], P(('vb', 'oj'), None, 'va')
- gamma_pair: float32 [3584, 8, 2048], P('va', 'oj', 'vb')
All inputs are finite; a program needn't handle non-finite values.
Results may differ from a plain program's by a relative error of at most 0.002.
Values may be sent and summed in bfloat16 or wider, within the bound.
A program may use at most 128 MiB of HBM per device.

v0:
```python
import jax
import jax.numpy as jnp
from jax import lax
from jax.sharding import PartitionSpec as P


def per_device(occ_slab, pair_slab, occ_energy, pair_energy, vir_energy):
    occ_full = lax.all_gather(occ_slab, ("vb", "oj"), axis=0, tiled=True)
    collected = lax.all_gather(pair_slab, "va", axis=0, tiled=True)
    mingled = lax.all_to_all(collected, "oj", split_axis=1, concat_axis=0, tiled=True)
    va_count = lax.axis_size("va")
    oj_count = lax.axis_size("oj")
    shaped = mingled.reshape(oj_count, va_count, -1, mingled.shape[1], mingled.shape[2])
    pair_full = jnp.swapaxes(shaped, 0, 1).reshape(-1, mingled.shape[1], mingled.shape[2])
    width_a = occ_full.shape[2]
    width_b = pair_full.shape[2]
    energy_a = lax.dynamic_slice_in_dim(vir_energy, lax.axis_index("va") * width_a, width_a)
    energy_b = lax.dynamic_slice_in_dim(vir_energy, lax.axis_index("vb") * width_b, width_b)
    pair_ints = jnp.einsum("qia,qjb->ijab", occ_full, pair_full, preferred_element_type=jnp.float32)
    denominator = (
        occ_energy[:, None, None, None]
        + pair_energy[None, :, None, None]
        - energy_a[None, None, :, None]
        - energy_b[None, None, None, :]
    )
    amplitudes = (pair_ints / denominator).astype(jnp.bfloat16)
    gamma_occ = lax.psum_scatter(
        jnp.einsum("ijab,qjb->qia", amplitudes, pair_full, preferred_element_type=jnp.float32),
        ("vb", "oj"),
        scatter_dimension=0,
        tiled=True,
    )
    gamma_pair = lax.psum_scatter(
        jnp.einsum("ijab,qia->qjb", amplitudes, occ_full, preferred_element_type=jnp.float32),
        "va",
        scatter_dimension=0,
        tiled=True,
    )
    return (gamma_occ, gamma_pair)


def solution(mesh):
    placed = (P(("vb", "oj"), None, "va"), P(("va", "oj"), None, "vb"), P(), P("oj"), P())
    return jax.shard_map(
        per_device,
        mesh=mesh,
        in_specs=placed,
        out_specs=(P(("vb", "oj"), None, "va"), P("va", "oj", "vb")),
        check_vma=False,
    )
```

profile of v0, /device:TPU:1, one launch (start us, length us, event | category | flops | bytes accessed | tf_op | source)
XLA Modules:
  0.0 833.1 jit_solution(16251034097933430811)
XLA Ops:
  7.2 0.0 all-gather.3.cloned.1.call-start
  7.2 1.9 copy.25
  9.1 0.0 all-gather.3.cloned.1.call-update
  9.2 0.0 all-gather.5.cloned.1.call-start
  9.2 1.6 copy.27
  10.8 0.0 all-gather.5.cloned.1.call-update
  10.8 0.0 copy-start.1
  10.8 103.1 %all-gather.3.cloned.1.call-done = bf16[448,8,512]{2,0,1:T(8,128)(2,1)} async-done(((bf16[56,8,512]{2,0,1:T(8,128)(2,1)}), bf16[448,8,512]{2,0,1:T(8,128)(2,1)}) %all-gather.3.cloned.1.call-update) | async-done | bytes 3670032 | tf_op jit(solution)/shard_map/all_gather | solution.py:9
  113.9 5.5 all-to-all-start
  119.4 0.0 all-reduce.7.cloned.1.call-start
  120.1 0.8 dynamic_slice.6
  120.8 0.8 dynamic_slice.7
  121.6 0.0 copy-done.1
  121.6 0.1 broadcast_subtract_fusion
  121.7 55.0 %all-to-all-done = bf16[448,8,512]{2,0,1:T(8,128)(2,1)} async-done(((bf16[448,8,512]{2,0,1:T(8,128)(2,1)}), bf16[448,8,512]{2,0,1:T(8,128)(2,1)}, u32[]{:S(2)}, u32[]{:S(2)}) %all-to-all-start) | async-done | bytes 3670048 | tf_op jit(solution)/shard_map/all_to_all | solution.py:10
  176.7 4.2 copy.26
  180.9 11.5 %all-gather.5.cloned.1.call-done = bf16[3584,2,256]{2,0,1:T(8,128)(2,1)} async-done(((bf16[112,2,256]{2,0,1:T(8,128)(2,1)}), bf16[3584,2,256]{2,0,1:T(8,128)(2,1)}) %all-gather.5.cloned.1.call-update) | async-done | bytes 3670032 | tf_op jit(solution)/shard_map/all_gather | solution.py:8
  192.5 0.0 copy-start
  192.5 5.4 fusion.2
  197.9 0.0 copy-done
  197.9 5.1 convolution_bitcast_fusion
  203.0 16.6 %copy.31 = f32[3584,1,512]{2,1,0:T(1,128)} copy(f32[3584,1,512]{0,2,1:T(8,128)} %convolution_bitcast_fusion) | data formatting | bytes 14680064 | tf_op jit(solution)/shard_map/ijab,qia->qjb/dot_general | solution.py:34
  219.6 0.0 all-reduce.7.cloned.1.call-update
  219.7 0.0 all-reduce.5.cloned.1.call-start
  219.7 7.1 convolution_bitcast_fusion.1
  226.8 11.7 %copy.30 = f32[3584,2,256]{2,1,0:T(2,128)} copy(f32[3584,2,256]{0,2,1:T(8,128)} %convolution_bitcast_fusion.1) | data formatting | bytes 14680064 | tf_op jit(solution)/shard_map/ijab,qjb->qia/dot_general | solution.py:28
  238.6 0.0 copy-start.3
  238.6 0.0 copy-start.2
  238.6 0.0 all-reduce.5.cloned.1.call-update
  238.6 0.6 copy-done.3
  239.2 0.6 dynamic-slice.2
  239.8 0.0 copy-done.2
  239.8 0.6 dynamic-slice
  241.7 289.5 %all-reduce.7.cloned.1.call-done = f32[3584,1,512]{2,1,0:T(1,128)} async-done(((f32[3584,1,512]{2,1,0:T(1,128)}), f32[3584,1,512]{2,1,0:T(1,128)}) %all-reduce.7.cloned.1.call-update) | async-done | bytes 7340048
  531.2 2.7 constant_dynamic-slice_fusion
  533.9 291.0 %all-reduce.5.cloned.1.call-done = f32[3584,2,256]{2,1,0:T(2,128)} async-done(((f32[3584,2,256]{2,1,0:T(2,128)}), f32[3584,2,256]{2,1,0:T(2,128)}) %all-reduce.5.cloned.1.call-update) | async-done | bytes 7340048
  824.9 1.6 constant_dynamic-slice_fusion.1
  (1 shorter events, 0.0 us)
Async XLA Ops:
  7.2 106.8 %all-gather.3.cloned.1.call-start = ((), (), s32[]{:S(2)}) async-start(), calls=%async_computation.1 | async-start | bytes 4128768 | tf_op jit(solution)/shard_map/all_gather | solution.py:9
  9.2 183.3 %all-gather.5.cloned.1.call-start = ((), (), s32[]{:S(2)}) async-start(), calls=%async_computation.2 | async-start | bytes 3784704 | tf_op jit(solution)/shard_map/all_gather | solution.py:8
  10.8 110.8 %copy-start.1 = (f32[2]{0:T(128)S(1)}, f32[2]{0:T(128)}, u32[]{:S(2)}) copy-start(f32[2]{0:T(128)} %param.7) | copy-start | bytes 28
  113.9 62.8 %all-to-all-start = ((bf16[448,8,512]{2,0,1:T(8,128)(2,1)}), bf16[448,8,512]{2,0,1:T(8,128)(2,1)}, u32[]{:S(2)}, u32[]{:S(2)}) async-start(bf16[448,8,512]{2,0,1:T(8,128)(2,1)} %all-gather.3.cloned.1.call-done), calls=%async_computation | async-start | bytes 7340032 | tf_op jit(solution)/shard_map/all_to_all | solution.py:10
  119.4 411.8 %all-reduce.7.cloned.1.call-start = ((), (), s32[]{:S(2)}) async-start(), calls=%async_computation.4 | async-start | bytes 14680064
  192.5 5.4 copy-start
  219.7 605.3 %all-reduce.5.cloned.1.call-start = ((), (), s32[]{:S(2)}) async-start(), calls=%async_computation.3 | async-start | bytes 14680064
  238.6 0.7 copy-start.3
  238.6 1.3 copy-start.2
Sparse Core Ops, SparseCore 0:
  11.1 102.7 all-gather.2
  116.3 76.1 all-gather.4
  219.8 311.3 all-reduce.6
  533.7 291.1 all-reduce.4
where the time goes:
time: 834 us; the launch traced here: 833 us
  waiting for transfers between devices  750 us (90%)
  local copies, waits for them, and re-layouts  43.8 us (5%)
  matrix products  17.6 us (2%)
  between operations  15.7 us (2%)
    unnamed x6, waiting for transfers between devices  581 us
    all_gather x1, waiting for transfers between devices, per_device(): collected = lax.all_gather(pair_slab, 'va', axis=0, tiled=True)  103 us
    all_to_all x1, waiting for transfers between devices, per_device(): lax.all_to_all(collected, 'oj', split_axis=1, concat_axis=0, tiled=True)  55 us
  transfers between devices with their start and end apart: 5, of which 5 were waited for; matrix products, arithmetic and copies ran while one was open for 4% of the time, Pallas kernels for 0%

commit v1 on v0

--- a/solution.py
+++ b/solution.py
@@ -4,10 +4,33 @@
 from jax.sharding import PartitionSpec as P
 
 
+def define_roots_here(frame_in, on_dim, dim_k=0):
+    plain = lax.axis_size("oj")
+    main, current_arr = (plain, lax.axis_index("oj"))
+    next_value = list(frame_in.shape)
+    part_next = frame_in.shape[on_dim] // main
+    next_value[on_dim] = part_next
+    y_new = next_value[dim_k]
+    next_value[dim_k] = y_new * main
+    state_now = jnp.zeros(next_value, frame_in.dtype)
+    for ii in range(main):
+        b_now = lax.dynamic_slice_in_dim(
+            frame_in, (current_arr ^ ii) * part_next, part_next, axis=on_dim
+        )
+        if ii:
+            b_now = lax.ppermute(
+                b_now, axis_name="oj", perm=list(map(lambda at: (at, at ^ ii), range(main)))
+            )
+        state_now = lax.dynamic_update_slice_in_dim(
+            state_now, b_now, (current_arr ^ ii) * y_new, axis=dim_k
+        )
+    return state_now
+
+
 def per_device(occ_slab, pair_slab, occ_energy, pair_energy, vir_energy):
     occ_full = lax.all_gather(occ_slab, ("vb", "oj"), axis=0, tiled=True)
     collected = lax.all_gather(pair_slab, "va", axis=0, tiled=True)
-    mingled = lax.all_to_all(collected, "oj", split_axis=1, concat_axis=0, tiled=True)
+    mingled = define_roots_here(collected, 1)
     va_count = lax.axis_size("va")
     oj_count = lax.axis_size("oj")
     shaped = mingled.reshape(oj_count, va_count, -1, mingled.shape[1], mingled.shape[2])

time: 834 us -> 700 us (0.84)
  waiting for transfers between devices: 750 us -> 602 us
    unnamed x6 -> x5, waiting for transfers between devices: 581 us -> 302 us
    reduce_scatter x0 -> x1, waiting for transfers between devices: none -> 144 us  [per_device(): lax.psum_scatter(jnp.einsum('ijab,qjb->qia', amplitudes, pair_full, prefe...]
    all_to_all x1 -> x0, waiting for transfers between devices: 55 us -> none  [per_device(): lax.all_to_all(collected, 'oj', split_axis=1, concat_axis=0, tiled=True)]
    ppermute x0 -> x7, waiting for transfers between devices: none -> 34.4 us  [define_roots_here(): lax.ppermute(b_now, axis_name='oj', perm=list(map(lambda at: (at, at ^ ii...]
    ppermute x0 -> x7, starting transfers between devices: none -> 13.4 us  [define_roots_here(): lax.ppermute(b_now, axis_name='oj', perm=list(map(lambda at: (at, at ^ ii...]
    dot_general x1 -> x0, local copies, waits for them, and re-layouts: 11.7 us -> none  [per_device(): jnp.einsum('ijab,qjb->qia', amplitudes, pair_full, preferred_element_type...]
    dynamic_update_slice x0 -> x7, local copies, waits for them, and re-layouts: none -> 9.85 us  [define_roots_here(): lax.dynamic_update_slice_in_dim(state_now, b_now, (current_arr ^ ii) * y_...]
  transfers between devices with their start and end apart: 5 -> 11, of which waited for: 5 -> 8; matrix products, arithmetic and copies ran while one was open for 4% -> 4% of each run, Pallas kernels for 0% -> 0%
where the time goes in v1:
time: 700 us; the launch traced here: 694 us
  waiting for transfers between devices  602 us (86%)
  local copies, waits for them, and re-layouts  46 us (7%)
  matrix products  17.6 us (3%)
  between operations  15.2 us (2%)
  starting transfers between devices  13.6 us (2%)
    unnamed x5, waiting for transfers between devices  302 us
    reduce_scatter x1, waiting for transfers between devices, per_device(): lax.psum_scatter(jnp.einsum('ijab,qjb->qia', amplitudes, pair_full, prefe...  144 us
    all_gather x1, waiting for transfers between devices, per_device(): collected = lax.all_gather(pair_slab, 'va', axis=0, tiled=True)  103 us
    ppermute x7, waiting for transfers between devices, define_roots_here(): lax.ppermute(b_now, axis_name='oj', perm=list(map(lambda at: (at, at ^ ii...  34.4 us
    all_gather x1, waiting for transfers between devices, per_device(): occ_full = lax.all_gather(occ_slab, ('vb', 'oj'), axis=0, tiled=True)  18.3 us
    dot_general x1, local copies, waits for them, and re-layouts, per_device(): jnp.einsum('ijab,qia->qjb', amplitudes, occ_full, preferred_element_type=...  16.7 us
  transfers between devices with their start and end apart: 11, of which 8 were waited for; matrix products, arithmetic and copies ran while one was open for 4% of the time, Pallas kernels for 0%

profile of v1, /device:TPU:1, one launch (start us, length us, event | category | flops | bytes accessed | tf_op | source)
XLA Modules:
  0.0 694.4 jit_solution(7591994752999357186)
XLA Ops:
  7.2 0.0 all-gather.3.cloned.1.call-start
  7.2 1.9 copy.25
  9.1 0.0 all-gather.3.cloned.1.call-update
  9.2 0.0 all-gather.5.cloned.1.call-start
  9.2 1.6 copy.27
  10.8 0.0 all-gather.5.cloned.1.call-update
  10.8 0.0 all-reduce.3.cloned.1.call-start
  10.9 103.1 %all-gather.3.cloned.1.call-done = bf16[448,8,512]{2,0,1:T(8,128)(2,1)} async-done(((bf16[56,8,512]{2,0,1:T(8,128)(2,1)}), bf16[448,8,512]{2,0,1:T(8,128)(2,1)}) %all-gather.3.cloned.1.call-update) | async-done | bytes 3670032 | tf_op jit(solution)/shard_map/all_gather | solution.py:32
  113.9 2.2 broadcast_in_dim.2
  116.1 1.2 copy-done
  117.3 1.1 constant_dynamic-slice_fusion
  118.4 1.1 collective-permute-start
  120.1 1.3 collective-permute-start.1
  121.4 0.8 dynamic_slice.38
  122.1 0.4 collective-permute-start.2
  122.6 2.7 collective-permute-start.3
  125.3 0.1 broadcast_subtract_fusion
  125.3 0.8 dynamic_slice.39
  126.1 0.7 collective-permute-start.4
  126.8 2.4 collective-permute-start.5
  129.2 1.8 constant_dynamic-update-slice_fusion.6
  131.1 5.6 collective-permute-done.1
  136.6 4.9 collective-permute-start.6
  141.5 1.9 constant_dynamic-update-slice_fusion.5
  143.4 10.2 %collective-permute-done.2 = bf16[448,1,512]{2,0,1:T(8,128)(2,1)} collective-permute-done((bf16[448,1,512]{2,0,1:T(8,128)(2,1)S(1)}, bf16[448,1,512]{2,0,1:T(8,128)(2,1)}, u32[]{:S(2)}, u32[]{:S(2)}) %collective-permute-start.2) | collective-permute-done | bytes 458784 | tf_op jit(solution)/shard_map/ppermute | solution.py:21
  153.6 1.9 constant_dynamic-update-slice_fusion.4
  155.4 10.5 %collective-permute-done.3 = bf16[448,1,512]{2,0,1:T(8,128)(2,1)} collective-permute-done((bf16[448,1,512]{2,0,1:T(8,128)(2,1)S(1)}, bf16[448,1,512]{2,0,1:T(8,128)(2,1)}, u32[]{:S(2)}, u32[]{:S(2)}) %collective-permute-start.3) | collective-permute-done | bytes 458784 | tf_op jit(solution)/shard_map/ppermute | solution.py:21
  165.9 1.8 constant_dynamic-update-slice_fusion.3
  167.7 8.2 %collective-permute-done.4 = bf16[448,1,512]{2,0,1:T(8,128)(2,1)S(1)} collective-permute-done((bf16[448,1,512]{2,0,1:T(8,128)(2,1)S(1)}, bf16[448,1,512]{2,0,1:T(8,128)(2,1)S(1)}, u32[]{:S(2)}, u32[]{:S(2)}) %collective-permute-start.4) | collective-permute-done | bytes 458784 | tf_op jit(solution)/shard_map/ppermute | solution.py:21
  175.9 0.8 constant_dynamic-update-slice_fusion.2
  176.7 0.0 collective-permute-done.5
  176.7 0.8 constant_dynamic-update-slice_fusion.1
  177.5 0.8 constant_dynamic-update-slice_fusion
  178.4 4.3 copy.26
  182.7 18.3 %all-gather.5.cloned.1.call-done = bf16[3584,2,256]{2,0,1:T(8,128)(2,1)} async-done(((bf16[112,2,256]{2,0,1:T(8,128)(2,1)}), bf16[3584,2,256]{2,0,1:T(8,128)(2,1)}) %all-gather.5.cloned.1.call-update) | async-done | bytes 3670032 | tf_op jit(solution)/shard_map/all_gather | solution.py:31
  201.0 5.4 fusion.2
  206.4 5.1 convolution_bitcast_fusion
  211.5 16.7 %copy.30 = f32[3584,1,512]{2,1,0:T(1,128)} copy(f32[3584,1,512]{0,2,1:T(8,128)} %convolution_bitcast_fusion) | data formatting | bytes 14680064 | tf_op jit(solution)/shard_map/ijab,qia->qjb/dot_general | solution.py:57
  228.2 0.0 all-reduce.3.cloned.1.call-update
  228.2 0.0 reduce-scatter.2.cloned.1.call-start
  228.3 7.0 %fusion.3 = f32[3584,2,256]{2,0,1:T(8,128)} fusion(bf16[3584,512,1]{1,0,2:T(8,128)(2,1)} %bitcast.35, bf16[2,256,512]{1,2,0:T(8,128)(2,1)S(1)} %fusion.2), kind=kOutput, calls=%fused_computation.23 | convolution fusion | flops 1879048192 | bytes 11534336 | tf_op jit(solution)/shard_map/ijab,qjb->qia/dot_general | solution.py:51
  235.3 0.0 reduce-scatter.2.cloned.1.call-update
  235.3 0.6 copy-done.3
  236.0 0.6 dynamic-slice
  237.2 302.4 %all-reduce.3.cloned.1.call-done = f32[3584,1,512]{2,1,0:T(1,128)} async-done(((f32[3584,1,512]{2,1,0:T(1,128)}), f32[3584,1,512]{2,1,0:T(1,128)}) %all-reduce.3.cloned.1.call-update) | async-done | bytes 7340048
  539.6 2.7 constant_dynamic-slice_fusion.7
  542.3 143.8 %reduce-scatter.2.cloned.1.call-done = f32[112,2,256]{2,0,1:T(8,128)} async-done(((f32[3584,2,256]{2,0,1:T(8,128)}), f32[112,2,256]{2,0,1:T(8,128)}) %reduce-scatter.2.cloned.1.call-update) | async-done | bytes 229392 | tf_op jit(solution)/shard_map/reduce_scatter | solution.py:50
  686.1 1.8 copy.31
  (9 shorter events, 0.0 us)
Async XLA Ops:
  7.2 106.8 %all-gather.3.cloned.1.call-start = ((), (), s32[]{:S(2)}) async-start(), calls=%async_computation.1 | async-start | bytes 4128768 | tf_op jit(solution)/shard_map/all_gather | solution.py:32
  9.2 191.8 %all-gather.5.cloned.1.call-start = ((), (), s32[]{:S(2)}) async-start(), calls=%async_computation.2 | async-start | bytes 3784704 | tf_op jit(solution)/shard_map/all_gather | solution.py:31
  10.8 528.8 %all-reduce.3.cloned.1.call-start = ((), (), s32[]{:S(2)}) async-start(), calls=%async_computation.4 | async-start | bytes 14680064
  113.9 3.4 copy-start
  117.3 4.1 copy-start.2
  118.4 8.4 %collective-permute-start = (bf16[448,1,512]{2,0,1:T(8,128)(2,1)S(1)}, bf16[448,1,512]{2,0,1:T(8,128)(2,1)}, u32[]{:S(2)}, u32[]{:S(2)}) collective-permute-start(bf16[448,1,512]{2,0,1:T(8,128)(2,1)S(1)} %get-tuple-element.16), channel_id=1, source_target_pairs={{0,1},{1,0},{2,3},{3,2},{4,5},{5,4},{6,7},{7,6},{8,9},{9,8},{10,11... | collective-permute-start | bytes 1376264 | tf_op jit(solution)/shard_map/ppermute | solution.py:21
  120.1 16.6 %collective-permute-start.1 = (bf16[448,1,512]{2,0,1:T(8,128)(2,1)S(1)}, bf16[448,1,512]{2,0,1:T(8,128)(2,1)}, u32[]{:S(2)}, u32[]{:S(2)}) collective-permute-start(bf16[448,1,512]{2,0,1:T(8,128)(2,1)S(1)} %get-tuple-element.15), channel_id=1, source_target_pairs={{0,2},{1,3},{2,0},{3,1},{4,6},{5,7},{6,4},{7,5},{8,10},{9,11},{10,... | collective-permute-start | bytes 1376264 | tf_op jit(solution)/shard_map/ppermute | solution.py:21
  122.1 31.4 %collective-permute-start.2 = (bf16[448,1,512]{2,0,1:T(8,128)(2,1)S(1)}, bf16[448,1,512]{2,0,1:T(8,128)(2,1)}, u32[]{:S(2)}, u32[]{:S(2)}) collective-permute-start(bf16[448,1,512]{2,0,1:T(8,128)(2,1)S(1)} %get-tuple-element.14), channel_id=1, source_target_pairs={{0,3},{1,2},{2,1},{3,0},{4,7},{5,6},{6,5},{7,4},{8,11},{9,10},{10,... | collective-permute-start | bytes 1376264 | tf_op jit(solution)/shard_map/ppermute | solution.py:21
  122.6 43.3 %collective-permute-start.3 = (bf16[448,1,512]{2,0,1:T(8,128)(2,1)S(1)}, bf16[448,1,512]{2,0,1:T(8,128)(2,1)}, u32[]{:S(2)}, u32[]{:S(2)}) collective-permute-start(bf16[448,1,512]{2,0,1:T(8,128)(2,1)S(1)} %get-tuple-element.13), channel_id=1, source_target_pairs={{0,4},{1,5},{2,6},{3,7},{4,0},{5,1},{6,2},{7,3},{8,12},{9,13},{10,... | collective-permute-start | bytes 1376264 | tf_op jit(solution)/shard_map/ppermute | solution.py:21
  126.1 49.8 %collective-permute-start.4 = (bf16[448,1,512]{2,0,1:T(8,128)(2,1)S(1)}, bf16[448,1,512]{2,0,1:T(8,128)(2,1)S(1)}, u32[]{:S(2)}, u32[]{:S(2)}) collective-permute-start(bf16[448,1,512]{2,0,1:T(8,128)(2,1)S(1)} %get-tuple-element.12), channel_id=1, source_target_pairs={{0,5},{1,4},{2,7},{3,6},{4,1},{5,0},{6,3},{7,2},{8,13},{9,12},{10,... | collective-permute-start | bytes 1376264 | tf_op jit(solution)/shard_map/ppermute | solution.py:21
  126.8 49.9 %collective-permute-start.5 = (bf16[448,1,512]{2,0,1:T(8,128)(2,1)S(1)}, bf16[448,1,512]{2,0,1:T(8,128)(2,1)S(1)}, u32[]{:S(2)}, u32[]{:S(2)}) collective-permute-start(bf16[448,1,512]{2,0,1:T(8,128)(2,1)S(1)} %get-tuple-element.11), channel_id=1, source_target_pairs={{0,6},{1,7},{2,4},{3,5},{4,2},{5,3},{6,0},{7,1},{8,14},{9,15},{10,... | collective-permute-start | bytes 1376264 | tf_op jit(solution)/shard_map/ppermute | solution.py:21
  136.6 40.9 %collective-permute-start.6 = (bf16[448,1,512]{2,0,1:T(8,128)(2,1)S(1)}, bf16[448,1,512]{2,0,1:T(8,128)(2,1)S(1)}, u32[]{:S(2)}, u32[]{:S(2)}) collective-permute-start(bf16[448,1,512]{2,0,1:T(8,128)(2,1)S(1)} %get-tuple-element.10), channel_id=1, source_target_pairs={{0,7},{1,6},{2,5},{3,4},{4,3},{5,2},{6,1},{7,0},{8,15},{9,14},{10,... | collective-permute-start | bytes 1376264 | tf_op jit(solution)/shard_map/ppermute | solution.py:21
  201.0 5.4 copy-start.1
  228.2 457.9 %reduce-scatter.2.cloned.1.call-start = ((), (), s32[]{:S(2)}) async-start(), calls=%async_computation.3 | async-start | bytes 7569408 | tf_op jit(solution)/shard_map/reduce_scatter | solution.py:50
  235.3 0.7 copy-start.3
Sparse Core Ops, SparseCore 0:
  11.1 102.7 all-gather.2
  116.3 84.6 all-gather.4
  228.3 311.2 all-reduce.2
  542.0 144.0 reduce-scatter.1
